TPU v7x, 256 devices: a whole 4x4x8 slice. The times are simulated.
256 devices in a mesh: branch: 4 (over y), leaf: 64 (over x, z, core).
Axes of the slice: x: 4, y: 4, z: 8, core: 2. Of those that a mesh axis runs over, the one named last changes fastest.
Arguments:
- charges: bfloat16 [262144, 128], P(('branch', 'leaf')), may hold values from -6 to 6
- near_src: int32 [4096, 12], P(('branch', 'leaf')), may hold values from 0 to 4095, as said below
- near_block: bfloat16 [4096, 64, 768], P(('branch', 'leaf')), may hold values from -0.21875 to 0.21875
- bases: bfloat16 [4096, 64, 128], P(('branch', 'leaf')), may hold values from -0.75 to 0.75
- transfers: bfloat16 [4096, 64, 128], P(('branch', 'leaf')), may hold values from -0.1875 to 0.1875
- couple: bfloat16 [4096, 64, 192], P(('branch', 'leaf')), may hold values from -0.75 to 0.75
- far_dev: int32 [4096, 3], P(('branch', 'leaf')), may hold values from 0 to 63, all different within a row; in each aligned block of 16 rows (0 to 15, 16 to 31, ...) at most 2 rows name the same one
- far_leaf: int32 [4096, 3], P(('branch', 'leaf')), may hold values from 0 to 15
- upper_couple: bfloat16 [256, 64, 128], P(('branch', 'leaf')), may hold values from -0.5 to 0.5
- upper_src: int32 [256, 2], P(('branch', 'leaf')), may hold values from 1 to 3
Outputs:
- potentials: bfloat16 [262144, 128], P(('branch', 'leaf'))
Inputs may be any that keep to these rules, and one draw needn't show every extreme that they name: near_src[s,k] lies in the same group of 1024 consecutive leaves as s and at most 8 leaves from s; that distance is reached. `far_dev`: within the rows of one device (aligned blocks of 16 rows), no value occurs more than 2 times, and some value occurs exactly 2 times.
All inputs are finite; a program needn't handle non-finite values.
Results may differ from a plain program's by a relative error of at most 0.0059.
Values may be sent and summed in bfloat16 or wider, within the bound.
A program may use at most 64 MiB of HBM per device.

v0:
```python
import jax
import jax.numpy as jnp
from jax import lax
from jax.sharding import PartitionSpec as P

LEAF = 64
RANK = 64
NEAR = 12
FAR = 3
HALO = 8
KU = 2


def with_halo(cells, sides, width):
    for axis, dim in sides:
        count = lax.axis_size(axis)
        ends = count - 1
        head = lax.slice_in_dim(cells, 0, width, axis=dim)
        tail = lax.slice_in_dim(cells, cells.shape[dim] - width, cells.shape[dim], axis=dim)
        cells = jnp.concatenate(
            [
                lax.ppermute(tail, axis, [(i, (i + 1) % count) for i in range(ends)]),
                cells,
                lax.ppermute(head, axis, [((i + 1) % count, i) for i in range(ends)]),
            ],
            axis=dim,
        )
    return cells


def per_device(
    charges,
    near_src,
    near_block,
    bases,
    transfers,
    couple,
    far_dev,
    far_leaf,
    upper_couple,
    upper_src,
):
    leaf_count = lax.axis_size("leaf")
    branch_count = lax.axis_size("branch")
    per_dev = charges.shape[0] // LEAF
    vectors = charges.shape[1]
    first = (lax.axis_index("branch") * leaf_count + lax.axis_index("leaf")) * per_dev
    local_points = charges.reshape(per_dev, LEAF, vectors)
    coeff = jnp.einsum(
        "lpr,lpn->lrn", bases[:, :, :RANK], local_points, preferred_element_type=jnp.float32
    ).astype(jnp.bfloat16)
    capacity = max(2, (3 * per_dev * FAR + 2 * leaf_count - 1) // (2 * leaf_count))
    padded = with_halo(charges, (("leaf", 0),), HALO * LEAF)
    padded = padded.reshape(per_dev + 2 * HALO, LEAF, vectors)
    local_src = near_src - (first - HALO)
    near_sum = jnp.zeros((per_dev, LEAF, vectors), jnp.float32)
    for column in range(NEAR):
        gathered = padded[local_src[:, column]]
        block = near_block[:, :, column * LEAF : (column + 1) * LEAF]
        near_sum = near_sum + jnp.einsum(
            "lps,lpn->lsn", block, gathered, preferred_element_type=jnp.float32
        )
    coupled = jnp.einsum(
        "lrkq,lrn->lkqn",
        couple.reshape(per_dev, RANK, FAR, RANK),
        coeff,
        preferred_element_type=jnp.float32,
    )
    coupled = coupled.astype(jnp.bfloat16).reshape(per_dev * FAR, RANK, vectors)
    owners = far_dev.reshape(-1)
    hits = (owners[:, None] == jnp.arange(leaf_count, dtype=jnp.int32)[None, :]).astype(jnp.int32)
    placed = jnp.sum((jnp.cumsum(hits, axis=0) - 1) * hits, axis=1)
    slots = owners * capacity + placed
    outgoing = (
        jnp.zeros((leaf_count * capacity, RANK, vectors), jnp.bfloat16).at[slots].set(coupled)
    )
    outgoing = outgoing.reshape(leaf_count, capacity, RANK, vectors)
    labels = (
        jnp.full((leaf_count * capacity,), per_dev, jnp.int32).at[slots].set(far_leaf.reshape(-1))
    )
    labels = labels.reshape(leaf_count, capacity)
    arrived, arrived_labels = (
        lax.all_to_all(outgoing, "leaf", split_axis=0, concat_axis=0, tiled=True),
        lax.all_to_all(labels, "leaf", split_axis=0, concat_axis=0, tiled=True),
    )
    select = (
        arrived_labels.reshape(1, -1) == jnp.arange(per_dev, dtype=jnp.int32)[:, None]
    ).astype(jnp.bfloat16)
    summed = jnp.dot(
        select,
        arrived.reshape(leaf_count * capacity, RANK * vectors),
        preferred_element_type=jnp.float32,
    )
    far_sum = summed.reshape(per_dev, RANK, vectors)
    parent_coeff = jnp.einsum(
        "lrq,lrn->qn", transfers[:, :, :RANK], coeff, preferred_element_type=jnp.float32
    ).astype(jnp.bfloat16)
    upper_blocks = upper_couple.reshape(RANK, KU, RANK)
    source_groups = (lax.axis_index("branch") + upper_src[0]) % branch_count
    everyone = lax.all_gather(parent_coeff[None], "branch", axis=0, tiled=True)
    parent_sum = jnp.zeros((RANK, vectors), jnp.float32)
    for column in range(KU):
        picked = lax.dynamic_index_in_dim(everyone, source_groups[column], 0, keepdims=False)
        parent_sum = parent_sum + jnp.einsum(
            "rq,rn->qn", upper_blocks[:, column, :], picked, preferred_element_type=jnp.float32
        )
    parent_down = parent_sum.astype(jnp.bfloat16)
    from_parent = jnp.einsum(
        "lrq,qn->lrn", transfers[:, :, RANK:], parent_down, preferred_element_type=jnp.float32
    )
    down = (far_sum + from_parent).astype(jnp.bfloat16)
    far_out = jnp.einsum(
        "lpr,lrn->lpn", bases[:, :, RANK:], down, preferred_element_type=jnp.float32
    )
    return (far_out + near_sum).astype(jnp.bfloat16).reshape(per_dev * LEAF, vectors)


def solution(mesh):
    in_specs = (
        P(("branch", "leaf"), None),
        P(("branch", "leaf"), None),
        P(("branch", "leaf"), None, None),
        P(("branch", "leaf"), None, None),
        P(("branch", "leaf"), None, None),
        P(("branch", "leaf"), None, None),
        P(("branch", "leaf"), None),
        P(("branch", "leaf"), None),
        P(("branch", "leaf"), None, None),
        P(("branch", "leaf"), None),
    )
    out_specs = P(("branch", "leaf"), None)
    return jax.shard_map(
        per_device, mesh=mesh, in_specs=in_specs, out_specs=out_specs, check_vma=False
    )
```

profile of v0, /device:TPU:1, one launch (start us, length us, event | category | flops | bytes accessed | tf_op | source)
XLA Modules:
  0.0 124.2 jit_solution(13020729972072253495)
XLA Ops:
  4.5 13.0 %all-to-all-start = ((s32[64,1,2]{2,1,0:T(1,128)}), s32[64,1,2]{2,1,0:T(1,128)S(1)}, u32[]{:S(2)}, u32[]{:S(2)}) async-start(s32[64,1,2]{2,1,0:T(1,128)} %bitcast.2), calls=%async_computation | async-start | bytes 65536 | tf_op jit(solution)/shard_map/all_to_all | solution.py:84
  17.4 1.6 %fusion.64 = (bf16[512,128]{1,0:T(8,128)(2,1)S(1)}, bf16[512,128]{1,0:T(8,128)(2,1)}) fusion(bf16[1024,128]{1,0:T(8,128)(2,1)} %param.10), kind=kLoop, calls=%fused_computation.123 | loop fusion | bytes 524288 | tf_op jit(solution)/shard_map/slice | solution.py:19
  19.1 2.4 %collective-permute-start.1 = (bf16[512,128]{1,0:T(8,128)(2,1)}, bf16[512,128]{1,0:T(8,128)(2,1)}, u32[]{:S(2)}, u32[]{:S(2)}) collective-permute-start(bf16[512,128]{1,0:T(8,128)(2,1)} %get-tuple-element.18), channel_id=1, source_target_pairs={{1,0},{2,1},{3,2},{4,3},{5,4},{6,5},{7,6},{8,7},{9,8},{10,9},{11,1... | collective-permute-start | bytes 393224 | tf_op jit(solution)/shard_map/ppermute | solution.py:24
  21.5 3.2 %collective-permute-start = (bf16[512,128]{1,0:T(8,128)(2,1)S(1)}, bf16[512,128]{1,0:T(8,128)(2,1)}, u32[]{:S(2)}, u32[]{:S(2)}) collective-permute-start(bf16[512,128]{1,0:T(8,128)(2,1)S(1)} %get-tuple-element.17), channel_id=1, source_target_pairs={{0,1},{1,2},{2,3},{3,4},{4,5},{5,6},{6,7},{7,8},{8,9},{9,10},{10,1... | collective-permute-start | bytes 393224 | tf_op jit(solution)/shard_map/ppermute | solution.py:22
  24.7 1.3 %convolution_convert_fusion = bf16[16,64,128]{2,1,0:T(8,128)(2,1)S(1)} fusion(bf16[16,64,128]{2,1,0:T(8,128)(2,1)} %bitcast.103, bf16[16,64,128]{2,1,0:T(8,128)(2,1)} %param.13), kind=kOutput, calls=%fused_computation.31 | convolution fusion | flops 16908288 | bytes 786432 | tf_op jit(solution)/shard_map/lpr,lpn->lrn/dot_general | solution.py:49
  29.0 9.5 %all-gather = bf16[256,128]{1,0:T(8,128)(2,1)S(1)} all-gather(bf16[64,128]{1,0:T(8,128)(2,1)S(1)} %fusion.7), channel_id=2, replica_groups=mesh['branch'=4,'leaf'=64] {'branch'}, dimensions={0}, use_global_device_ids=true | all-gather | bytes 81920 | tf_op jit(solution)/shard_map/all_gather | solution.py:100
  40.2 1.9 %broadcast_in_dim.7 = bf16[128,64,128]{2,1,0:T(8,128)(2,1)} broadcast(bf16[]{:T(256)} %constant.47.clone.1), dimensions={} | broadcast | bytes 2097154 | tf_op jit(solution)/shard_map/broadcast_in_dim | solution.py:75
  42.1 6.2 %scatter_fusion = bf16[128,64,128]{2,1,0:T(8,128)(2,1)} fusion(bf16[128,64,128]{2,1,0:T(8,128)(2,1)} %broadcast_in_dim.7, s32[48]{0:T(128)S(1)} %fusion.58, bf16[48,64,128]{2,1,0:T(8,128)(2,1)S(1)} %bitcast.102), kind=kCustom, calls=%fused_computation.13 | custom fusion | bytes 2359488 | tf_op jit(solution)/shard_map/scatter | solution.py:75
  49.0 12.1 %all-to-all-start.1 = ((bf16[64,2,64,128]{3,2,1,0:T(8,128)(2,1)}), bf16[64,2,64,128]{3,2,1,0:T(8,128)(2,1)S(1)}, u32[]{:S(2)}, u32[]{:S(2)}) async-start(bf16[64,2,64,128]{3,2,1,0:T(8,128)(2,1)} %bitcast.10), calls=%async_computation.1 | async-start | bytes 4194304 | tf_op jit(solution)/shard_map/all_to_all | solution.py:83
  69.2 1.4 %gather_fusion.1 = bf16[16,64,128]{2,1,0:T(8,128)(2,1)} fusion(bf16[32,64,128]{2,1,0:T(8,128)(2,1)S(1)} %bitcast.86, s32[1024]{0:T(1024)} %get-tuple-element.32), kind=kCustom, calls=%fused_computation.1 | custom fusion | bytes 524352 | tf_op jit(solution)/shard_map/gather | solution.py:58
  73.2 1.4 %gather_fusion.3 = bf16[16,64,128]{2,1,0:T(8,128)(2,1)} fusion(bf16[32,64,128]{2,1,0:T(8,128)(2,1)S(1)} %bitcast.89, s32[1024]{0:T(1024)} %get-tuple-element.30), kind=kCustom, calls=%fused_computation.3 | custom fusion | bytes 524352 | tf_op jit(solution)/shard_map/gather | solution.py:58
  75.9 1.4 %gather_fusion.5 = bf16[16,64,128]{2,1,0:T(8,128)(2,1)} fusion(bf16[32,64,128]{2,1,0:T(8,128)(2,1)S(1)} %bitcast.91, s32[1024]{0:T(1024)} %get-tuple-element.28), kind=kCustom, calls=%fused_computation.5 | custom fusion | bytes 524352 | tf_op jit(solution)/shard_map/gather | solution.py:58
  77.3 1.4 %gather_fusion.6 = bf16[16,64,128]{2,1,0:T(8,128)(2,1)} fusion(bf16[32,64,128]{2,1,0:T(8,128)(2,1)S(1)} %bitcast.92, s32[1024]{0:T(1024)} %get-tuple-element.27), kind=kCustom, calls=%fused_computation.6 | custom fusion | bytes 524352 | tf_op jit(solution)/shard_map/gather | solution.py:58
  78.7 1.4 %gather_fusion.7 = bf16[16,64,128]{2,1,0:T(8,128)(2,1)} fusion(bf16[32,64,128]{2,1,0:T(8,128)(2,1)S(1)} %bitcast.93, s32[1024]{0:T(1024)} %get-tuple-element.26), kind=kCustom, calls=%fused_computation.7 | custom fusion | bytes 524352 | tf_op jit(solution)/shard_map/gather | solution.py:58
  80.1 1.4 %gather_fusion.8 = bf16[16,64,128]{2,1,0:T(8,128)(2,1)} fusion(bf16[32,64,128]{2,1,0:T(8,128)(2,1)S(1)} %bitcast.94, s32[1024]{0:T(1024)} %get-tuple-element.25), kind=kCustom, calls=%fused_computation.8 | custom fusion | bytes 524352 | tf_op jit(solution)/shard_map/gather | solution.py:58
  82.2 1.4 %gather_fusion.10 = bf16[16,64,128]{2,1,0:T(8,128)(2,1)} fusion(bf16[32,64,128]{2,1,0:T(8,128)(2,1)S(1)} %bitcast.96, s32[1024]{0:T(1024)} %get-tuple-element.23), kind=kCustom, calls=%fused_computation.10 | custom fusion | bytes 524352 | tf_op jit(solution)/shard_map/gather | solution.py:58
  84.9 1.6 %fusion.21 = f32[16,128,64]{1,2,0:T(8,128)S(1)} fusion(bf16[16,64,128]{2,1,0:T(8,128)(2,1)} %gather_fusion.1, bf16[16,64,768]{2,1,0:T(8,128)(2,1)} %param.12), kind=kOutput, calls=%fused_computation.52 | convolution fusion | flops 16777216 | bytes 1048576 | tf_op jit(solution)/shard_map/lps,lpn->lsn/dot_general | solution.py:60
  86.5 1.4 %convolution_add_fusion.10 = f32[16,128,64]{1,2,0:T(8,128)S(1)} fusion(f32[16,128,64]{1,2,0:T(8,128)S(1)} %fusion.21, bf16[16,64,128]{2,1,0:T(8,128)(2,1)} %gather_fusion, bf16[16,64,768]{2,1,0:T(8,128)(2,1)} %param.12), kind=kOutput, calls=%fused_computation.28 | convolution fusion | flops 16908288 | bytes 1572864 | tf_op jit(solution)/shard_map/lps,lpn->lsn/dot_general | solution.py:60
  92.0 20.4 %all-to-all-done.1 = bf16[64,2,64,128]{3,2,1,0:T(8,128)(2,1)S(1)} async-done(((bf16[64,2,64,128]{3,2,1,0:T(8,128)(2,1)}), bf16[64,2,64,128]{3,2,1,0:T(8,128)(2,1)S(1)}, u32[]{:S(2)}, u32[]{:S(2)}) %all-to-all-start.1) | async-done | bytes 2097184 | tf_op jit(solution)/shard_map/all_to_all | solution.py:83
  112.4 3.2 %copy.142 = bf16[16,8,64,128]{3,1,2,0:T(8,128)(2,1)} copy(bf16[16,8,64,128]{3,2,1,0:T(8,128)(2,1)S(1)} %bitcast.98) | data formatting | bytes 4194304
  115.5 3.2 %copy.94 = bf16[8192,128]{1,0:T(8,128)(2,1)S(1)} copy(bf16[8192,128]{0,1:T(8,128)(2,1)} %bitcast.100) | data formatting | bytes 4194304 | tf_op jit(solution)/shard_map/dot_general | solution.py:89
  118.8 1.4 %fusion.54 = f32[16,64,128]{2,0,1:T(8,128)} fusion(bf16[64,128,128]{2,1,0:T(8,128)(2,1)S(1)} %bitcast.99, s32[128]{0:T(128)S(1)} %copy-done.16), kind=kOutput, calls=%fused_computation.96 | convolution fusion | flops 33556480 | bytes 2621952 | tf_op jit(solution)/shard_map/dot_general | solution.py:89
  120.2 1.6 %fusion.3 = bf16[16,64,128]{2,0,1:T(8,128)(2,1)S(1)} fusion(f32[16,64,128]{2,0,1:T(8,128)} %fusion.54, f32[128,64]{0,1:T(8,128)S(1)} %fusion.32, bf16[16,64,64]{2,1,0:T(8,128)(2,1)} %slice.108, bf16[64,1,64]{2,1,0:T(2,128)(2,1)S(1)} %get-tuple-element.19, bf16[4,64,128]{2,1,0:T(8,128)(2,1)S(1)} %bitcast.105, s32[]{:T(128)S(6)} %select_n.76), kind=kOutput, calls=%fused_computation.30 | convolution fusion | flops 18104320 | bytes 999428 | tf_op jit(solution)/shard_map/lrq,qn->lrn/dot_general | solution.py:108
  122.1 2.1 %fusion.2 = bf16[16,128,64]{1,2,0:T(8,128)(2,1)} fusion(f32[16,128,64]{1,2,0:T(8,128)S(1)} %fusion.9, f32[16,128,64]{1,2,0:T(8,128)S(1)} %convolution_add_fusion.1, bf16[16,64,128]{2,1,0:T(8,128)(2,1)S(1)} %copy-done.3, bf16[16,64,768]{2,1,0:T(8,128)(2,1)} %param.12), kind=kOutput, calls=%fused_computation.29 | convolution fusion | flops 17170432 | bytes 1835008 | tf_op jit(solution)/shard_map/lps,lpn->lsn/dot_general | solution.py:60
  (89 shorter events, 23.7 us)
Async XLA Ops:
  0.0 26.0 %copy-start = (bf16[16,64,192]{2,1,0:T(8,128)(2,1)S(1)}, bf16[16,64,192]{2,1,0:T(8,128)(2,1)}, u32[]{:S(2)}) copy-start(bf16[16,64,192]{2,1,0:T(8,128)(2,1)} %param.15) | copy-start | bytes 1179652
  4.5 44.5 %all-to-all-start = ((s32[64,1,2]{2,1,0:T(1,128)}), s32[64,1,2]{2,1,0:T(1,128)S(1)}, u32[]{:S(2)}, u32[]{:S(2)}) async-start(s32[64,1,2]{2,1,0:T(1,128)} %bitcast.2), calls=%async_computation | async-start | bytes 65536 | tf_op jit(solution)/shard_map/all_to_all | solution.py:84
  19.1 49.1 %collective-permute-start.1 = (bf16[512,128]{1,0:T(8,128)(2,1)}, bf16[512,128]{1,0:T(8,128)(2,1)}, u32[]{:S(2)}, u32[]{:S(2)}) collective-permute-start(bf16[512,128]{1,0:T(8,128)(2,1)} %get-tuple-element.18), channel_id=1, source_target_pairs={{1,0},{2,1},{3,2},{4,3},{5,4},{6,5},{7,6},{8,7},{9,8},{10,9},{11,1... | collective-permute-start | bytes 393224 | tf_op jit(solution)/shard_map/ppermute | solution.py:24
  21.5 46.7 %collective-permute-start = (bf16[512,128]{1,0:T(8,128)(2,1)S(1)}, bf16[512,128]{1,0:T(8,128)(2,1)}, u32[]{:S(2)}, u32[]{:S(2)}) collective-permute-start(bf16[512,128]{1,0:T(8,128)(2,1)S(1)} %get-tuple-element.17), channel_id=1, source_target_pairs={{0,1},{1,2},{2,3},{3,4},{4,5},{5,6},{6,7},{7,8},{8,9},{9,10},{10,1... | collective-permute-start | bytes 393224 | tf_op jit(solution)/shard_map/ppermute | solution.py:22
  24.7 1.8 %copy-start.13 = (bf16[16,64,128]{2,1,0:T(8,128)(2,1)S(1)}, bf16[16,64,128]{2,1,0:T(8,128)(2,1)}, u32[]{:S(2)}) copy-start(bf16[16,64,128]{2,1,0:T(8,128)(2,1)} %param.14) | copy-start | bytes 786436
  26.0 0.7 copy-start.17
  26.0 1.4 %copy-start.15 = (s32[16,12]{1,0:T(8,128)S(1)}, s32[16,12]{1,0:T(8,128)}, u32[]{:S(2)}) copy-start(s32[16,12]{1,0:T(8,128)} %param.11) | copy-start | bytes 2308
  26.5 12.2 %copy-start.14 = (bf16[1,64,128]{2,1,0:T(8,128)(2,1)S(1)}, bf16[1,64,128]{2,1,0:T(8,128)(2,1)}, u32[]{:S(2)}) copy-start(bf16[1,64,128]{2,1,0:T(8,128)(2,1)} %param.18) | copy-start | bytes 49156
  49.0 19.2 %copy-start.2 = (bf16[1024,128]{1,0:T(8,128)(2,1)S(1)}, bf16[1024,128]{1,0:T(8,128)(2,1)}, u32[]{:S(2)}) copy-start(bf16[1024,128]{1,0:T(8,128)(2,1)} %param.10) | copy-start | bytes 786436
  49.0 63.3 %all-to-all-start.1 = ((bf16[64,2,64,128]{3,2,1,0:T(8,128)(2,1)}), bf16[64,2,64,128]{3,2,1,0:T(8,128)(2,1)S(1)}, u32[]{:S(2)}, u32[]{:S(2)}) async-start(bf16[64,2,64,128]{3,2,1,0:T(8,128)(2,1)} %bitcast.10), calls=%async_computation.1 | async-start | bytes 4194304 | tf_op jit(solution)/shard_map/all_to_all | solution.py:83
  84.9 2.9 %copy-start.1 = (bf16[16,64,768]{2,1,0:T(8,128)(2,1)S(1)}, bf16[16,64,768]{2,1,0:T(8,128)(2,1)}, u32[]{:S(2)}) copy-start(bf16[16,64,768]{2,1,0:T(8,128)(2,1)} %param.12) | copy-start | bytes 4718596
  84.9 3.0 %copy-start.12 = (bf16[16,64,128]{2,1,0:T(8,128)(2,1)S(1)}, bf16[16,64,128]{2,1,0:T(8,128)(2,1)}, u32[]{:S(2)}) copy-start(bf16[16,64,128]{2,1,0:T(8,128)(2,1)} %gather_fusion.2) | copy-start | bytes 786436
  86.5 1.7 %copy-start.10 = (bf16[16,64,128]{2,1,0:T(8,128)(2,1)S(1)}, bf16[16,64,128]{2,1,0:T(8,128)(2,1)}, u32[]{:S(2)}) copy-start(bf16[16,64,128]{2,1,0:T(8,128)(2,1)} %gather_fusion.3) | copy-start | bytes 786436
  87.9 1.0 copy-start.11
  88.2 1.0 copy-start.8
  88.8 1.0 copy-start.9
  89.1 1.0 copy-start.6
  89.8 1.0 copy-start.7
  90.7 0.9 copy-start.5
  115.5 3.2 %copy-start.16 = (s32[128]{0:T(128)S(1)}, s32[128]{0:T(128)}, u32[]{:S(2)}) copy-start(s32[128]{0:T(128)} %eq.36) | copy-start | bytes 1540
  118.7 3.1 %copy-start.4 = (bf16[16,64,128]{2,1,0:T(8,128)(2,1)S(1)}, bf16[16,64,128]{2,1,0:T(8,128)(2,1)}, u32[]{:S(2)}) copy-start(bf16[16,64,128]{2,1,0:T(8,128)(2,1)} %param.13) | copy-start | bytes 786436
  120.2 1.9 %copy-start.3 = (bf16[16,64,128]{2,1,0:T(8,128)(2,1)S(1)}, bf16[16,64,128]{2,1,0:T(8,128)(2,1)}, u32[]{:S(2)}) copy-start(bf16[16,64,128]{2,1,0:T(8,128)(2,1)} %gather_fusion.11) | copy-start | bytes 786436
where the time goes:
time: 125 us; the launch traced here: 124 us
  local copies, waits for them, and re-layouts  39.2 us (31%)
  starting transfers between devices  30.6 us (24%)
  waiting for transfers between devices  20.4 us (16%)
  matrix products  13.4 us (11%)
  blocking collectives  9.52 us (8%)
  other arithmetic  6.4 us (5%)
  between operations  4.58 us (4%)
    all_to_all x1, waiting for transfers between devices, per_device(): lax.all_to_all(outgoing, 'leaf', split_axis=0, concat_axis=0, tiled=True)  20.4 us
    gather x12, local copies, waits for them, and re-layouts, per_device(): gathered = padded[local_src[:, column]]  15.7 us
    all_to_all x1, starting transfers between devices, per_device(): lax.all_to_all(labels, 'leaf', split_axis=0, concat_axis=0, tiled=True)  13 us
    all_to_all x1, starting transfers between devices, per_device(): lax.all_to_all(outgoing, 'leaf', split_axis=0, concat_axis=0, tiled=True)  12.1 us
    all_gather x1, blocking collectives, per_device(): everyone = lax.all_gather(parent_coeff[None], 'branch', axis=0, tiled=True)  9.52 us
    dot_general x12, matrix products, per_device(): jnp.einsum('lps,lpn->lsn', block, gathered, preferred_element_type=jnp.fl...  7.91 us
    scatter x1, local copies, waits for them, and re-layouts, per_device(): jnp.zeros((leaf_count * capacity, RANK, vectors), jnp.bfloat16).at[slots]  6.22 us
    unnamed x39, local copies, waits for them, and re-layouts  5.82 us
  transfers between devices with their start and end apart: 4, of which 1 were waited for; matrix products, arithmetic and copies ran while one was open for 34% of the time, Pallas kernels for 0%

commit v1 on v0

v1 whole, which is shorter than its diff:
```python
import jax
import jax.numpy as jnp
from jax import lax
from jax.experimental import pallas as pl
from jax.experimental.pallas import tpu as pltpu
from jax.sharding import PartitionSpec as P

LEAF = 64
RANK = 64
NRHS = 128
LEAF_DEV = 16
NEAR = 12
FAR = 3
HALO = 8
KU = 2
PAIRS = LEAF_DEV * FAR
EMPTY = PAIRS * 32 + LEAF_DEV
MESH = pl.DeviceIdType.MESH
BF = jnp.bfloat16
F32 = jnp.float32


def tdot(a, b):
    return lax.dot_general(a, b, (((0,), (0,)), ((), ())), preferred_element_type=F32)


def dot(a, b):
    return jnp.dot(a, b, preferred_element_type=F32)


def step_of(i):
    far = 4 - (i + 1) // 2
    return far if i % 2 == 1 or i == 0 else -far


def kernel(
    fd, fl, ns, us, charges, near_block, bases, transfers, couple, upper,
    out,
    pad, nb, bv, tv, cv, uv, coeff, cpl, idxv, idxs, lab, labr, xs, xr, vrow, zs, zr, pcs, pcr,
    down_from_parent, near, downs,
    load_sem, idx_sem, halo_ss, halo_rs, lab_ss, lab_rs, pc_ss, pc_rs, xs_sem, xr_sem, zs_sem, zr_sem,
):
    b = lax.axis_index("branch")
    me = lax.axis_index("leaf")
    c = me % 2
    z = (me // 2) % 8
    x = me // 16
    g = x * 2 + c
    left = (b, (me + 63) % 64)
    right = (b, (me + 1) % 64)
    up = (b, (x * 8 + (z + 1) % 8) * 2 + c)
    low = (b, (x * 8 + (z + 7) % 8) * 2 + c)

    def member(k):
        other = (g + k) % 8
        return other, (b, ((other // 2) * 8 + z) * 2 + other % 2)

    def group(k):
        return ((b + k) % 4, me)

    mine = pad.at[pl.ds(HALO, LEAF_DEV)]
    loads = [
        pltpu.make_async_copy(src, dst, load_sem.at[n])
        for n, (src, dst) in enumerate(
            [(charges, mine), (bases, bv), (couple, cv), (transfers, tv), (upper, uv), (near_block, nb)]
        )
    ]
    for load in loads:
        load.start()

    barrier = pltpu.get_barrier_semaphore()
    partners = [member(k)[1] for k in range(1, 8)] + [up, low, left, right] + [group(k) for k in range(1, 4)]
    for partner in partners:
        pl.semaphore_signal(barrier, inc=1, device_id=partner, device_id_type=MESH)

    lane = lax.broadcasted_iota(jnp.int32, (8, 128), 1)
    row = lax.broadcasted_iota(jnp.int32, (8, 128), 0)
    one = jnp.full((8, 128), EMPTY, jnp.int32)
    two = jnp.full((8, 128), EMPTY, jnp.int32)
    for t in range(LEAF_DEV):
        for k in range(FAR):
            code = (t * FAR + k) * 32 + fl[t, k]
            hit = lane == fd[t, k]
            taken = one != EMPTY
            two = jnp.where(hit & taken, code, two)
            one = jnp.where(hit & ~taken, code, one)
    code = jnp.where(row == 0, one, jnp.where(row == 1, two, EMPTY))
    idxv[...] = code >> 5
    to_scalars = pltpu.make_async_copy(idxv, idxs, idx_sem)
    to_scalars.start()
    lab[...] = (code & 31).astype(F32)

    loads[0].wait()
    loads[1].wait()

    def coeff_step(t, carry):
        coeff[t] = tdot(bv[t], pad[t + HALO])[:RANK].astype(BF)
        return carry

    lax.fori_loop(0, LEAF_DEV, coeff_step, 0, unroll=True)

    pl.semaphore_wait(barrier, len(partners))

    def halo_copy(n):
        src = pad.at[pl.ds(LEAF_DEV if n == 0 else HALO, HALO)]
        dst = pad.at[pl.ds(0 if n == 0 else HALO + LEAF_DEV, HALO)]
        return pltpu.make_async_remote_copy(
            src, dst, halo_ss.at[n], halo_rs.at[n], device_id=(right, left)[n], device_id_type=MESH
        )

    for n in range(2):
        halo_copy(n).start()

    def lab_copy(k):
        return pltpu.make_async_remote_copy(
            lab, labr.at[g], lab_ss, lab_rs, device_id=member(k)[1], device_id_type=MESH
        )

    def lab_step(k, carry):
        lab_copy(k).start()
        return carry

    lax.fori_loop(1, 8, lab_step, 0)
    labr[g] = lab[...]

    loads[2].wait()

    def couple_step(t, carry):
        product = tdot(cv[t], coeff[t]).astype(BF)
        cpl[pl.ds(t * FAR, FAR)] = product.reshape(FAR, 4, 16, NRHS)
        return carry

    lax.fori_loop(0, LEAF_DEV, couple_step, 0, unroll=True)
    cpl[PAIRS] = jnp.zeros((4, 16, NRHS), BF)
    to_scalars.wait()

    def z_of(i):
        return (z + step_of(i) + 8) % 8

    def fill(i):
        def fill_step(other, carry):
            device = ((other // 2) * 8 + z_of(i)) * 2 + other % 2
            for slot in range(2):
                xs[other, i, :, slot * 16:(slot + 1) * 16, :] = cpl[idxs[slot, device]]
            return carry

        lax.fori_loop(0, 8, fill_step, 0, unroll=True)
        xr[i, :, g] = xs[g, i]

    def send_x(i, h):
        def send_step(k, carry):
            other, target = member(k)
            pltpu.make_async_remote_copy(
                xs.at[other, i, pl.ds(2 * h, 2)],
                xr.at[i, pl.ds(2 * h, 2), g],
                xs_sem,
                xr_sem.at[i, h],
                device_id=target,
                device_id_type=MESH,
            ).start()
            return carry

        lax.fori_loop(1, 8, send_step, 0, unroll=True)

    rounds = [(0,), (1, 2), (3, 4), (5, 6), (7,)]
    for chunks in rounds:
        for i in chunks:
            fill(i)
        for h in range(2):
            for i in chunks:
                send_x(i, h)

    loads[3].wait()
    packed = tdot(tv[...].reshape(LEAF_DEV * RANK, 2 * RANK), coeff[...].reshape(LEAF_DEV * RANK, NRHS))
    pcs[...] = packed[:RANK].astype(BF)

    def pc_copy(k):
        return pltpu.make_async_remote_copy(
            pcs, pcr.at[3 - k], pc_ss.at[k - 1], pc_rs.at[3 - k], device_id=group(k), device_id_type=MESH
        )

    for k in range(1, 4):
        pc_copy(k).start()

    pltpu.make_async_copy(labr.at[pl.ds(0, 7)], labr.at[pl.ds(0, 7)], lab_rs).wait()
    spread_row = lax.broadcasted_iota(jnp.int32, (64, 256), 0)
    spread_col = lax.broadcasted_iota(jnp.int32, (64, 256), 1)
    spread = (spread_row // 8 == spread_col // 32) & (spread_row % 8 == (spread_col // 16) % 2)
    by_device = tdot(labr[...].reshape(64, 128).astype(BF), spread.astype(F32).astype(BF)).astype(BF)
    chunk = lax.broadcasted_iota(jnp.int32, (16, 128), 0)
    far = 4 - (chunk + 1) // 2
    chunk_z = (z + jnp.where(chunk % 2 == 1, far, -far) + 16) % 8
    pick = lax.broadcasted_iota(jnp.int32, (16, 128), 1) == (x * 8 + chunk_z) * 2 + c
    labels = dot(pick.astype(F32).astype(BF), by_device)
    column = lax.broadcasted_iota(jnp.int32, (16, 256), 1)
    vrow[...] = labels * 16.0 + (column % 16).astype(F32)

    first = (b * 64 + me) * LEAF_DEV - HALO

    def near_step(s, carry):
        tall = jnp.concatenate([nb[s, :, 128 * j:128 * (j + 1)] for j in range(NEAR // 2)], axis=0)
        even = jnp.concatenate([pad[(ns[s, 2 * j] - first) & 31] for j in range(NEAR // 2)], axis=0)
        odd = jnp.concatenate([pad[(ns[s, 2 * j + 1] - first) & 31] for j in range(NEAR // 2)], axis=0)
        both = tdot(tall, jnp.concatenate([even, odd], axis=1))
        near[s] = both[:LEAF, :NRHS] + both[LEAF:, NRHS:]
        return carry

    def parents():
        loads[4].wait()
        for k in range(1, 4):
            pc_copy(k).wait_recv()
        picked = jnp.concatenate([pcr[jnp.clip(us[0, k] - 1, 0, 2)] for k in range(KU)], axis=1)
        both = tdot(uv[0], picked)
        parent_down = (both[:RANK, :NRHS] + both[RANK:, NRHS:]).astype(BF)
        lifted = jnp.concatenate([jnp.zeros((RANK, NRHS), BF), parent_down], axis=0)
        down_from_parent[...] = dot(tv[...].reshape(LEAF_DEV * RANK, 2 * RANK), lifted).reshape(
            LEAF_DEV, 4, 16, NRHS
        )

    tall_row = lax.broadcasted_iota(jnp.int32, (256, 256), 0).astype(F32)

    def slots(i, h):
        region = xr.at[i, pl.ds(2 * h, 2), pl.ds(0, 7)]
        pltpu.make_async_copy(region, region, xr_sem.at[i, h]).wait()
        hot = jnp.where(tall_row == vrow[i:i + 1, :], 1.0, 0.0).astype(BF)
        blocks = jnp.concatenate([xr[i, 2 * h + q].reshape(256, NRHS) for q in range(2)], axis=1)
        sums = dot(hot, blocks)
        return [sums[:, q * NRHS:(q + 1) * NRHS] for q in range(2)]

    def z_copy(i, h, sign):
        rows = pl.ds(0, 256) if i else pl.ds(0 if sign > 0 else 128, 128)
        place = 7 if i == 0 and sign < 0 else i
        return pltpu.make_async_remote_copy(
            zs.at[i, h, :, rows],
            zr.at[i, h, :, rows],
            zs_sem.at[place, h],
            zr_sem.at[place, h],
            device_id=up if sign > 0 else low,
            device_id_type=MESH,
        )

    def unit(i, h):
        sums = slots(i, h)
        if i == 0:
            for q in range(2):
                zs[i, h, q] = sums[q].astype(BF)
            z_copy(i, h, 1).start()
            z_copy(i, h, -1).start()
            return
        if i == 7:
            z_copy(5, h, 1).wait_recv()
            z_copy(6, h, -1).wait_recv()
            for q in range(2):
                total = sums[q] + zr[5, h, q].astype(F32) + zr[6, h, q].astype(F32)
                total = total.reshape(LEAF_DEV, 16, NRHS) + down_from_parent[:, 2 * h + q]
                downs[:, 2 * h + q] = total.astype(BF)
            return
        sign = 1 if i % 2 else -1
        before = max(i - 2, 0)
        z_copy(before, h, sign).wait_recv()
        for q in range(2):
            if before:
                zs[i, h, q] = (sums[q] + zr[before, h, q].astype(F32)).astype(BF)
            else:
                met = slice(0, 128) if sign > 0 else slice(128, 256)
                rest = slice(128, 256) if sign > 0 else slice(0, 128)
                zs[i, h, q, met] = (sums[q][met] + zr[0, h, q, met].astype(F32)).astype(BF)
                zs[i, h, q, rest] = sums[q][rest].astype(BF)
        z_copy(i, h, sign).start()

    unit(0, 0)
    unit(0, 1)
    for n in range(2):
        halo_copy(n).wait_recv()
    loads[5].wait()
    done = 0
    for chunks in rounds[1:4]:
        for h in range(2):
            for i in chunks:
                unit(i, h)
                if done == 0:
                    parents()
                if done < 8:
                    lax.fori_loop(2 * done, 2 * done + 2, near_step, 0, unroll=True)
                done += 1

    sent = xs.at[pl.ds(0, 7)]
    unit(7, 0)
    unit(7, 1)

    def out_step(s, carry):
        down = downs[s].reshape(RANK, NRHS)
        lifted = jnp.concatenate([jnp.zeros((RANK, NRHS), BF), down], axis=0)
        out[s] = (dot(bv[s], lifted) + near[s]).astype(BF)
        return carry

    lax.fori_loop(0, LEAF_DEV, out_step, 0, unroll=True)

    pltpu.make_async_copy(sent, sent, xs_sem).wait()
    for n in range(2):
        halo_copy(n).wait_send()
    pltpu.make_async_copy(labr.at[pl.ds(0, 7)], labr.at[pl.ds(0, 7)], lab_ss).wait()
    for k in range(1, 4):
        pc_copy(k).wait_send()
    for h in range(2):
        z_copy(0, h, -1).wait_send()
        for i in range(7):
            z_copy(i, h, 1 if i == 0 or i % 2 else -1).wait_send()


def per_device(
    charges, near_src, near_block, bases, transfers, couple, far_dev, far_leaf, upper_couple, upper_src
):
    smem = pl.BlockSpec(memory_space=pltpu.SMEM)
    hbm = pl.BlockSpec(memory_space=pl.ANY)
    dma = pltpu.SemaphoreType.DMA
    out = pl.pallas_call(
        kernel,
        name="adjoint",
        out_shape=jax.ShapeDtypeStruct((LEAF_DEV, LEAF, NRHS), BF),
        in_specs=[smem] * 4 + [hbm] * 6,
        out_specs=pl.BlockSpec(memory_space=pltpu.VMEM),
        scratch_shapes=[
            pltpu.VMEM((LEAF_DEV + 2 * HALO, LEAF, NRHS), BF),
            pltpu.VMEM((LEAF_DEV, LEAF, NEAR * LEAF), BF),
            pltpu.VMEM((LEAF_DEV, LEAF, 2 * RANK), BF),
            pltpu.VMEM((LEAF_DEV, RANK, 2 * RANK), BF),
            pltpu.VMEM((LEAF_DEV, RANK, FAR * RANK), BF),
            pltpu.VMEM((1, RANK, KU * RANK), BF),
            pltpu.VMEM((LEAF_DEV, RANK, NRHS), BF),
            pltpu.VMEM((PAIRS + 1, 4, 16, NRHS), BF),
            pltpu.VMEM((8, 128), jnp.int32),
            pltpu.SMEM((8, 128), jnp.int32),
            pltpu.VMEM((8, 128), F32),
            pltpu.VMEM((8, 8, 128), F32),
            pltpu.VMEM((8, 8, 4, 32, NRHS), BF),
            pltpu.VMEM((8, 4, 8, 32, NRHS), BF),
            pltpu.VMEM((16, 256), F32),
            pltpu.VMEM((7, 2, 2, 256, NRHS), BF),
            pltpu.VMEM((7, 2, 2, 256, NRHS), BF),
            pltpu.VMEM((RANK, NRHS), BF),
            pltpu.VMEM((3, RANK, NRHS), BF),
            pltpu.VMEM((LEAF_DEV, 4, 16, NRHS), F32),
            pltpu.VMEM((LEAF_DEV, LEAF, NRHS), F32),
            pltpu.VMEM((LEAF_DEV, 4, 16, NRHS), BF),
            dma((6,)),
            dma,
            dma((2,)),
            dma((2,)),
            dma,
            dma,
            dma((3,)),
            dma((3,)),
            dma,
            dma((8, 2)),
            dma((8, 2)),
            dma((8, 2)),
        ],
        compiler_params=pltpu.CompilerParams(
            collective_id=0, has_side_effects=True, vmem_limit_bytes=56 * 1024 * 1024
        ),
    )(
        far_dev, far_leaf, near_src, upper_src,
        charges.reshape(LEAF_DEV, LEAF, NRHS), near_block, bases, transfers, couple, upper_couple,
    )
    return out.reshape(LEAF_DEV * LEAF, NRHS)


def solution(mesh):
    rows = P(("branch", "leaf"), None)
    blocks = P(("branch", "leaf"), None, None)
    in_specs = (rows, rows, blocks, blocks, blocks, blocks, rows, rows, blocks, rows)
    return jax.shard_map(per_device, mesh=mesh, in_specs=in_specs, out_specs=rows, check_vma=False)
```

time: 125 us -> 44.5 us (0.36)
  Pallas kernels: 0 us -> 39.9 us
  local copies, waits for them, and re-layouts: 39.2 us -> 4.37 us
  starting transfers between devices: 30.6 us -> 0 us
  waiting for transfers between devices: 20.4 us -> 0 us
  matrix products: 13.4 us -> 0 us
  blocking collectives: 9.52 us -> 0 us
  other arithmetic: 6.4 us -> 0 us
  between operations: 4.58 us -> 0.01 us
    pallas_call x0 -> x1, Pallas kernels: none -> 39.9 us  [per_device(): pl.pallas_call(kernel, name='adjoint', out_shape=jax.ShapeDtypeStruct((LE...]
    all_to_all x2 -> x0, starting transfers between devices: 25.1 us -> none  [the longest x1 13 us: per_device(): lax.all_to_all(labels, 'leaf', split_axis=0, concat_axis=0, tiled=True)]
    all_to_all x2 -> x0, waiting for transfers between devices: 20.4 us -> none  [the longest x1 20.4 us: per_device(): lax.all_to_all(outgoing, 'leaf', split_axis=0, concat_axis=0, tiled=True)]
    gather x12 -> x0, local copies, waits for them, and re-layouts: 15.7 us -> none  [per_device(): gathered = padded[local_src[:, column]]]
    dot_general x18 -> x0, matrix products: 13 us -> none  [the longest x12 7.91 us: per_device(): jnp.einsum('lps,lpn->lsn', block, gathered, preferred_element_type=jnp.fl...]
    all_gather x1 -> x0, blocking collectives: 9.52 us -> none  [per_device(): everyone = lax.all_gather(parent_coeff[None], 'branch', axis=0, tiled=True)]
    scatter x2 -> x0, local copies, waits for them, and re-layouts: 6.95 us -> none  [the longest x1 6.22 us: per_device(): jnp.zeros((leaf_count * capacity, RANK, vectors), jnp.bfloat16).at[slots]]
    ppermute x2 -> x0, starting transfers between devices: 5.55 us -> none  [the longest x1 3.2 us: with_halo(): lax.ppermute(tail, axis, [(i, (i + 1) % count) for i in range(ends)])]
  transfers between devices with their start and end apart: 4 -> 0, of which waited for: 1 -> 0; matrix products, arithmetic and copies ran while one was open for 34% -> 0% of each run, Pallas kernels for 0% -> 0%
where the time goes in v1:
time: 44.5 us; the launch traced here: 44.3 us
  Pallas kernels  39.9 us (90%)
  local copies, waits for them, and re-layouts  4.37 us (10%)
    pallas_call x1, Pallas kernels, per_device(): pl.pallas_call(kernel, name='adjoint', out_shape=jax.ShapeDtypeStruct((LE...  39.9 us
    unnamed x3, local copies, waits for them, and re-layouts  4.37 us

profile of v1, /device:TPU:1, one launch (start us, length us, event | category | flops | bytes accessed | tf_op | source)
XLA Modules:
  0.0 44.3 jit_solution(387155884056498858)
XLA Ops:
  0.0 1.4 %copy.11.fd = s32[16,3]{1,0:T(8,128)} copy(s32[16,3]{0,1:T(4,128)} %param.16) | data formatting | bytes 384 | tf_op args[6]
  1.4 1.3 %copy.12.fl = s32[16,3]{1,0:T(8,128)} copy(s32[16,3]{0,1:T(4,128)} %param.17) | data formatting | bytes 384 | tf_op args[7]
  2.7 39.9 %adjoint.1 = bf16[16,64,128]{2,1,0:T(8,128)(2,1)} custom-call(s32[16,3]{1,0:T(8,128)} %copy.11.fd, s32[16,3]{1,0:T(8,128)} %copy.12.fl, s32[16,12]{1,0:T(8,128)} %ns.1, s32[1,2]{1,0:T(1,128)} %us.1, bf16[16,64,128]{2,1,0:T(8,128)(2,1)} %bitcast.3, bf16[16,64,768]{2,1,0:T(8,128)(2,1)} %near_block.1, bf16[16,64,128]{2,1,0:T(8,128)(2,1)} %bases.1, ...), custom_call_target="tpu_custom_call" | custom-call | tf_op jit(solution)/shard_map/adjoint/pallas_call | solution.py:317
  42.6 1.7 %copy.14 = bf16[1024,128]{1,0:T(8,128)(2,1)} copy(bf16[1024,128]{1,0:T(8,128)(2,1)} %bitcast.2) | data formatting | bytes 524288

commit v2 on v1

--- a/solution.py
+++ b/solution.py
@@ -34,9 +34,9 @@
 
 
 def kernel(
-    fd, fl, ns, us, charges, near_block, bases, transfers, couple, upper,
+    fd_hbm, fl_hbm, ns_hbm, us_hbm, charges, near_block, bases, transfers, couple, upper,
     out,
-    pad, nb, bv, tv, cv, uv, coeff, cpl, idxv, idxs, lab, labr, xs, xr, vrow, zs, zr, pcs, pcr,
+    fd, fl, ns, us, pad, nb, bv, tv, cv, uv, coeff, cpl, idxv, idxs, lab, labr, xs, xr, vrow, zs, zr, pcs, pcr,
     down_from_parent, near, downs,
     load_sem, idx_sem, halo_ss, halo_rs, lab_ss, lab_rs, pc_ss, pc_rs, xs_sem, xr_sem, zs_sem, zr_sem,
 ):
@@ -58,29 +58,34 @@
     def group(k):
         return ((b + k) % 4, me)
 
+    barrier = pltpu.get_barrier_semaphore()
+    partners = [member(k)[1] for k in range(1, 8)] + [up, low, left, right] + [group(k) for k in range(1, 4)]
+    for partner in partners:
+        pl.semaphore_signal(barrier, inc=1, device_id=partner, device_id_type=MESH)
+
     mine = pad.at[pl.ds(HALO, LEAF_DEV)]
     loads = [
         pltpu.make_async_copy(src, dst, load_sem.at[n])
         for n, (src, dst) in enumerate(
-            [(charges, mine), (bases, bv), (couple, cv), (transfers, tv), (upper, uv), (near_block, nb)]
+            [
+                (charges, mine), (bases, bv), (couple, cv), (transfers, tv), (upper, uv), (near_block, nb),
+                (fd_hbm, fd), (fl_hbm, fl), (ns_hbm, ns), (us_hbm, us),
+            ]
         )
     ]
-    for load in loads:
-        load.start()
-
-    barrier = pltpu.get_barrier_semaphore()
-    partners = [member(k)[1] for k in range(1, 8)] + [up, low, left, right] + [group(k) for k in range(1, 4)]
-    for partner in partners:
-        pl.semaphore_signal(barrier, inc=1, device_id=partner, device_id_type=MESH)
-
+    for n in (6, 7, 0, 1, 2):
+        loads[n].start()
+
+    loads[6].wait()
+    loads[7].wait()
     lane = lax.broadcasted_iota(jnp.int32, (8, 128), 1)
     row = lax.broadcasted_iota(jnp.int32, (8, 128), 0)
     one = jnp.full((8, 128), EMPTY, jnp.int32)
     two = jnp.full((8, 128), EMPTY, jnp.int32)
     for t in range(LEAF_DEV):
         for k in range(FAR):
-            code = (t * FAR + k) * 32 + fl[t, k]
-            hit = lane == fd[t, k]
+            code = (t * FAR + k) * 32 + fl[k, t]
+            hit = lane == fd[k, t]
             taken = one != EMPTY
             two = jnp.where(hit & taken, code, two)
             one = jnp.where(hit & ~taken, code, one)
@@ -163,12 +168,18 @@
         lax.fori_loop(1, 8, send_step, 0, unroll=True)
 
     rounds = [(0,), (1, 2), (3, 4), (5, 6), (7,)]
-    for chunks in rounds:
+
+    def issue(chunks):
         for i in chunks:
             fill(i)
         for h in range(2):
             for i in chunks:
                 send_x(i, h)
+
+    issue(rounds[0])
+    issue(rounds[1])
+    for n in (3, 4, 5, 8, 9):
+        loads[n].start()
 
     loads[3].wait()
     packed = tdot(tv[...].reshape(LEAF_DEV * RANK, 2 * RANK), coeff[...].reshape(LEAF_DEV * RANK, NRHS))
@@ -207,6 +218,7 @@
 
     def parents():
         loads[4].wait()
+        loads[9].wait()
         for k in range(1, 4):
             pc_copy(k).wait_recv()
         picked = jnp.concatenate([pcr[jnp.clip(us[0, k] - 1, 0, 2)] for k in range(KU)], axis=1)
@@ -270,11 +282,15 @@
 
     unit(0, 0)
     unit(0, 1)
+    issue(rounds[2])
     for n in range(2):
         halo_copy(n).wait_recv()
     loads[5].wait()
+    loads[8].wait()
     done = 0
-    for chunks in rounds[1:4]:
+    for n, chunks in enumerate(rounds[1:4]):
+        if n < 2:
+            issue(rounds[n + 3])
         for h in range(2):
             for i in chunks:
                 unit(i, h)
@@ -311,16 +327,19 @@
 def per_device(
     charges, near_src, near_block, bases, transfers, couple, far_dev, far_leaf, upper_couple, upper_src
 ):
-    smem = pl.BlockSpec(memory_space=pltpu.SMEM)
-    hbm = pl.BlockSpec(memory_space=pl.ANY)
+    hbm = pl.BlockSpec(memory_space=pltpu.HBM)
     dma = pltpu.SemaphoreType.DMA
     out = pl.pallas_call(
         kernel,
         name="adjoint",
-        out_shape=jax.ShapeDtypeStruct((LEAF_DEV, LEAF, NRHS), BF),
-        in_specs=[smem] * 4 + [hbm] * 6,
+        out_shape=pltpu.VMEM((LEAF_DEV, LEAF, NRHS), BF),
+        in_specs=[hbm] * 10,
         out_specs=pl.BlockSpec(memory_space=pltpu.VMEM),
         scratch_shapes=[
+            pltpu.SMEM((FAR, LEAF_DEV), jnp.int32),
+            pltpu.SMEM((FAR, LEAF_DEV), jnp.int32),
+            pltpu.SMEM((LEAF_DEV, NEAR), jnp.int32),
+            pltpu.SMEM((1, KU), jnp.int32),
             pltpu.VMEM((LEAF_DEV + 2 * HALO, LEAF, NRHS), BF),
             pltpu.VMEM((LEAF_DEV, LEAF, NEAR * LEAF), BF),
             pltpu.VMEM((LEAF_DEV, LEAF, 2 * RANK), BF),
@@ -343,7 +362,7 @@
             pltpu.VMEM((LEAF_DEV, 4, 16, NRHS), F32),
             pltpu.VMEM((LEAF_DEV, LEAF, NRHS), F32),
             pltpu.VMEM((LEAF_DEV, 4, 16, NRHS), BF),
-            dma((6,)),
+            dma((10,)),
             dma,
             dma((2,)),
             dma((2,)),
@@ -357,11 +376,16 @@
             dma((8, 2)),
         ],
         compiler_params=pltpu.CompilerParams(
-            collective_id=0, has_side_effects=True, vmem_limit_bytes=56 * 1024 * 1024
+            collective_id=0, has_side_effects=True, vmem_limit_bytes=24 * 1024 * 1024
         ),
     )(
-        far_dev, far_leaf, near_src, upper_src,
-        charges.reshape(LEAF_DEV, LEAF, NRHS), near_block, bases, transfers, couple, upper_couple,
+        *[
+            pltpu.with_memory_space_constraint(a, pltpu.HBM)
+            for a in (
+                far_dev.T, far_leaf.T, near_src, upper_src,
+                charges.reshape(LEAF_DEV, LEAF, NRHS), near_block, bases, transfers, couple, upper_couple,
+            )
+        ]
     )
     return out.reshape(LEAF_DEV * LEAF, NRHS)
 

time: 44.5 us -> 38.8 us (0.87)
  local copies, waits for them, and re-layouts: 4.37 us -> 0.71 us
  Pallas kernels: 39.9 us -> 38 us
    unnamed x3 -> x1, local copies, waits for them, and re-layouts: 4.37 us -> 0.71 us
    pallas_call x1, Pallas kernels: 39.9 us -> 38 us  [per_device(): pl.pallas_call(kernel, name='adjoint', out_shape=pltpu.VMEM((LEAF_DEV, LE...]
where the time goes in v2:
time: 38.8 us; the launch traced here: 38.7 us
  Pallas kernels  38 us (98%)
  local copies, waits for them, and re-layouts  0.71 us (2%)
    pallas_call x1, Pallas kernels, per_device(): pl.pallas_call(kernel, name='adjoint', out_shape=pltpu.VMEM((LEAF_DEV, LE...  38 us

profile of v2, /device:TPU:1, one launch (start us, length us, event | category | flops | bytes accessed | tf_op | source)
XLA Modules:
  0.0 38.7 jit_solution(5149730620303795733)
XLA Ops:
  0.0 38.0 %adjoint.1 = bf16[16,64,128]{2,1,0:T(8,128)(2,1)S(1)} custom-call(s32[3,16]{1,0:T(4,128)} %bitcast.6, s32[3,16]{1,0:T(4,128)} %bitcast.7, s32[16,12]{1,0:T(8,128)} %ns_hbm.1, s32[1,2]{1,0:T(1,128)} %us_hbm.1, bf16[16,64,128]{2,1,0:T(8,128)(2,1)} %bitcast.5, bf16[16,64,768]{2,1,0:T(8,128)(2,1)} %near_block.1, bf16[16,64,128]{2,1,0:T(8,128)(2,1)} %bases.1, ...), custom_call_target="tpu_custom_call" | custom-call | tf_op jit(solution)/shard_map/adjoint/pallas_call | solution.py:332
  38.0 0.7 %copy.12 = bf16[1024,128]{1,0:T(8,128)(2,1)} copy(bf16[1024,128]{1,0:T(8,128)(2,1)S(1)} %bitcast.4) | data formatting | bytes 524288

commit v3 on v2

--- a/solution.py
+++ b/solution.py
@@ -38,7 +38,7 @@
     out,
     fd, fl, ns, us, pad, nb, bv, tv, cv, uv, coeff, cpl, idxv, idxs, lab, labr, xs, xr, vrow, zs, zr, pcs, pcr,
     down_from_parent, near, downs,
-    load_sem, idx_sem, halo_ss, halo_rs, lab_ss, lab_rs, pc_ss, pc_rs, xs_sem, xr_sem, zs_sem, zr_sem,
+    load_sem, idx_sem, halo_ss, halo_rs, lab_ss, lab_rs, pc_ss, pc_rs, xs_sem, xr_sem, zs_sem, zr_sem, later_sem,
 ):
     b = lax.axis_index("branch")
     me = lax.axis_index("leaf")
@@ -59,9 +59,14 @@
         return ((b + k) % 4, me)
 
     barrier = pltpu.get_barrier_semaphore()
-    partners = [member(k)[1] for k in range(1, 8)] + [up, low, left, right] + [group(k) for k in range(1, 4)]
+    partners = [member(k)[1] for k in range(1, 8)] + [up, low, left, right]
     for partner in partners:
         pl.semaphore_signal(barrier, inc=1, device_id=partner, device_id_type=MESH)
+    for k in range(1, 4):
+
+        @pl.when(b + k < 4)
+        def _():
+            pl.semaphore_signal(barrier, inc=1, device_id=group(k), device_id_type=MESH)
 
     mine = pad.at[pl.ds(HALO, LEAF_DEV)]
     loads = [
@@ -104,7 +109,13 @@
 
     lax.fori_loop(0, LEAF_DEV, coeff_step, 0, unroll=True)
 
-    pl.semaphore_wait(barrier, len(partners))
+    pl.semaphore_wait(barrier, len(partners) + b)
+    for k in range(1, 4):
+
+        @pl.when(b + k >= 4)
+        def _():
+            pl.semaphore_signal(later_sem, inc=1, device_id=group(k), device_id_type=MESH)
+
 
     def halo_copy(n):
         src = pad.at[pl.ds(LEAF_DEV if n == 0 else HALO, HALO)]
@@ -189,6 +200,10 @@
         return pltpu.make_async_remote_copy(
             pcs, pcr.at[3 - k], pc_ss.at[k - 1], pc_rs.at[3 - k], device_id=group(k), device_id_type=MESH
         )
+
+    @pl.when(b < 3)
+    def _():
+        pl.semaphore_wait(later_sem, 3 - b)
 
     for k in range(1, 4):
         pc_copy(k).start()
@@ -374,6 +389,7 @@
             dma((8, 2)),
             dma((8, 2)),
             dma((8, 2)),
+            pltpu.SemaphoreType.REGULAR,
         ],
         compiler_params=pltpu.CompilerParams(
             collective_id=0, has_side_effects=True, vmem_limit_bytes=24 * 1024 * 1024

time: 38.8 us -> 37.8 us (0.974)
  Pallas kernels: 38 us -> 37 us
    pallas_call x1, Pallas kernels: 38 us -> 37 us  [per_device(): pl.pallas_call(kernel, name='adjoint', out_shape=pltpu.VMEM((LEAF_DEV, LE...]
where the time goes in v3:
time: 37.8 us; the launch traced here: 37.7 us
  Pallas kernels  37 us (98%)
  local copies, waits for them, and re-layouts  0.71 us (2%)
    pallas_call x1, Pallas kernels, per_device(): pl.pallas_call(kernel, name='adjoint', out_shape=pltpu.VMEM((LEAF_DEV, LE...  37 us

profile of v3, /device:TPU:1, one launch (start us, length us, event | category | flops | bytes accessed | tf_op | source)
XLA Modules:
  0.0 37.7 jit_solution(11944549777075898434)
XLA Ops:
  0.0 37.0 %adjoint.1 = bf16[16,64,128]{2,1,0:T(8,128)(2,1)S(1)} custom-call(s32[3,16]{1,0:T(4,128)} %bitcast.6, s32[3,16]{1,0:T(4,128)} %bitcast.7, s32[16,12]{1,0:T(8,128)} %ns_hbm.1, s32[1,2]{1,0:T(1,128)} %us_hbm.1, bf16[16,64,128]{2,1,0:T(8,128)(2,1)} %bitcast.5, bf16[16,64,768]{2,1,0:T(8,128)(2,1)} %near_block.1, bf16[16,64,128]{2,1,0:T(8,128)(2,1)} %bases.1, ...), custom_call_target="tpu_custom_call" | custom-call | tf_op jit(solution)/shard_map/adjoint/pallas_call | solution.py:347
  37.0 0.7 %copy.12 = bf16[1024,128]{1,0:T(8,128)(2,1)} copy(bf16[1024,128]{1,0:T(8,128)(2,1)S(1)} %bitcast.4) | data formatting | bytes 524288

commit v4 on v3

--- a/solution.py
+++ b/solution.py
@@ -15,6 +15,7 @@
 KU = 2
 PAIRS = LEAF_DEV * FAR
 EMPTY = PAIRS * 32 + LEAF_DEV
+TURNS = [(2, 1), (3, 1), (1, 1), (2, 0), (3, 0), (1, 0), (0, 1)]
 MESH = pl.DeviceIdType.MESH
 BF = jnp.bfloat16
 F32 = jnp.float32
@@ -52,7 +53,8 @@
     low = (b, (x * 8 + (z + 7) % 8) * 2 + c)
 
     def member(k):
-        other = (g + k) % 8
+        ahead, flip = TURNS[k - 1]
+        other = ((x + ahead) % 4) * 2 + (c + flip) % 2
         return other, (b, ((other // 2) * 8 + z) * 2 + other % 2)
 
     def group(k):
@@ -132,11 +134,8 @@
             lab, labr.at[g], lab_ss, lab_rs, device_id=member(k)[1], device_id_type=MESH
         )
 
-    def lab_step(k, carry):
+    for k in range(1, 8):
         lab_copy(k).start()
-        return carry
-
-    lax.fori_loop(1, 8, lab_step, 0)
     labr[g] = lab[...]
 
     loads[2].wait()
@@ -164,7 +163,7 @@
         xr[i, :, g] = xs[g, i]
 
     def send_x(i, h):
-        def send_step(k, carry):
+        for k in range(1, 8):
             other, target = member(k)
             pltpu.make_async_remote_copy(
                 xs.at[other, i, pl.ds(2 * h, 2)],
@@ -174,9 +173,6 @@
                 device_id=target,
                 device_id_type=MESH,
             ).start()
-            return carry
-
-        lax.fori_loop(1, 8, send_step, 0, unroll=True)
 
     rounds = [(0,), (1, 2), (3, 4), (5, 6), (7,)]
 

time: 37.8 us -> 37.2 us (0.984)
  Pallas kernels: 37 us -> 36.3 us
    pallas_call x1, Pallas kernels: 37 us -> 36.3 us  [per_device(): pl.pallas_call(kernel, name='adjoint', out_shape=pltpu.VMEM((LEAF_DEV, LE...]
where the time goes in v4:
time: 37.2 us; the launch traced here: 37 us
  Pallas kernels  36.3 us (98%)
  local copies, waits for them, and re-layouts  0.71 us (2%)
    pallas_call x1, Pallas kernels, per_device(): pl.pallas_call(kernel, name='adjoint', out_shape=pltpu.VMEM((LEAF_DEV, LE...  36.3 us

profile of v4, /device:TPU:1, one launch (start us, length us, event | category | flops | bytes accessed | tf_op | source)
XLA Modules:
  0.0 37.0 jit_solution(934430632678874569)
XLA Ops:
  0.0 36.3 %adjoint.1 = bf16[16,64,128]{2,1,0:T(8,128)(2,1)S(1)} custom-call(s32[3,16]{1,0:T(4,128)} %bitcast.6, s32[3,16]{1,0:T(4,128)} %bitcast.7, s32[16,12]{1,0:T(8,128)} %ns_hbm.1, s32[1,2]{1,0:T(1,128)} %us_hbm.1, bf16[16,64,128]{2,1,0:T(8,128)(2,1)} %bitcast.5, bf16[16,64,768]{2,1,0:T(8,128)(2,1)} %near_block.1, bf16[16,64,128]{2,1,0:T(8,128)(2,1)} %bases.1, ...), custom_call_target="tpu_custom_call" | custom-call | tf_op jit(solution)/shard_map/adjoint/pallas_call | solution.py:343
  36.3 0.7 %copy.12 = bf16[1024,128]{1,0:T(8,128)(2,1)} copy(bf16[1024,128]{1,0:T(8,128)(2,1)S(1)} %bitcast.4) | data formatting | bytes 524288

commit v5 on v4

--- a/solution.py
+++ b/solution.py
@@ -126,8 +126,6 @@
             src, dst, halo_ss.at[n], halo_rs.at[n], device_id=(right, left)[n], device_id_type=MESH
         )
 
-    for n in range(2):
-        halo_copy(n).start()
 
     def lab_copy(k):
         return pltpu.make_async_remote_copy(
@@ -136,6 +134,8 @@
 
     for k in range(1, 8):
         lab_copy(k).start()
+    for n in range(2):
+        halo_copy(n).start()
     labr[g] = lab[...]
 
     loads[2].wait()
@@ -315,13 +315,16 @@
     unit(7, 0)
     unit(7, 1)
 
+    nothing = jnp.zeros((RANK, NRHS), BF)
+
     def out_step(s, carry):
-        down = downs[s].reshape(RANK, NRHS)
-        lifted = jnp.concatenate([jnp.zeros((RANK, NRHS), BF), down], axis=0)
-        out[s] = (dot(bv[s], lifted) + near[s]).astype(BF)
+        pair = [jnp.concatenate([nothing, downs[2 * s + n].reshape(RANK, NRHS)], axis=0) for n in range(2)]
+        both = dot(bv[pl.ds(2 * s, 2)].reshape(2 * LEAF, 2 * RANK), jnp.concatenate(pair, axis=1))
+        out[2 * s] = (both[:LEAF, :NRHS] + near[2 * s]).astype(BF)
+        out[2 * s + 1] = (both[LEAF:, NRHS:] + near[2 * s + 1]).astype(BF)
         return carry
 
-    lax.fori_loop(0, LEAF_DEV, out_step, 0, unroll=True)
+    lax.fori_loop(0, LEAF_DEV // 2, out_step, 0, unroll=True)
 
     pltpu.make_async_copy(sent, sent, xs_sem).wait()
     for n in range(2):

time: 37.2 us -> 37.2 us (level)
  no operation moved by 1% of the time
where the time goes in v5:
time: 37.2 us; the launch traced here: 37.1 us
  Pallas kernels  36.4 us (98%)
  local copies, waits for them, and re-layouts  0.71 us (2%)
    pallas_call x1, Pallas kernels, per_device(): pl.pallas_call(kernel, name='adjoint', out_shape=pltpu.VMEM((LEAF_DEV, LE...  36.4 us

profile of v5, /device:TPU:1, one launch (start us, length us, event | category | flops | bytes accessed | tf_op | source)
XLA Modules:
  0.0 37.1 jit_solution(2174859756866248171)
XLA Ops:
  0.0 36.4 %adjoint.1 = bf16[16,64,128]{2,1,0:T(8,128)(2,1)S(1)} custom-call(s32[3,16]{1,0:T(4,128)} %bitcast.6, s32[3,16]{1,0:T(4,128)} %bitcast.7, s32[16,12]{1,0:T(8,128)} %ns_hbm.1, s32[1,2]{1,0:T(1,128)} %us_hbm.1, bf16[16,64,128]{2,1,0:T(8,128)(2,1)} %bitcast.5, bf16[16,64,768]{2,1,0:T(8,128)(2,1)} %near_block.1, bf16[16,64,128]{2,1,0:T(8,128)(2,1)} %bases.1, ...), custom_call_target="tpu_custom_call" | custom-call | tf_op jit(solution)/shard_map/adjoint/pallas_call | solution.py:346
  36.4 0.7 %copy.12 = bf16[1024,128]{1,0:T(8,128)(2,1)} copy(bf16[1024,128]{1,0:T(8,128)(2,1)S(1)} %bitcast.4) | data formatting | bytes 524288

commit v6 on v5

--- a/solution.py
+++ b/solution.py
@@ -37,7 +37,7 @@
 def kernel(
     fd_hbm, fl_hbm, ns_hbm, us_hbm, charges, near_block, bases, transfers, couple, upper,
     out,
-    fd, fl, ns, us, pad, nb, bv, tv, cv, uv, coeff, cpl, idxv, idxs, lab, labr, xs, xr, vrow, zs, zr, pcs, pcr,
+    fd, fl, ns, us, pad, nb, bv, tv, cv, uv, coeff, cpl, idxv, idxs, lab, labr, xs, xr, vrow, hots, zs, zr, pcs, pcr,
     down_from_parent, near, downs,
     load_sem, idx_sem, halo_ss, halo_rs, lab_ss, lab_rs, pc_ss, pc_rs, xs_sem, xr_sem, zs_sem, zr_sem, later_sem,
 ):
@@ -216,6 +216,9 @@
     labels = dot(pick.astype(F32).astype(BF), by_device)
     column = lax.broadcasted_iota(jnp.int32, (16, 256), 1)
     vrow[...] = labels * 16.0 + (column % 16).astype(F32)
+    tall_row = lax.broadcasted_iota(jnp.int32, (256, 256), 0).astype(F32)
+    for i in range(8):
+        hots[i] = jnp.where(tall_row == vrow[i:i + 1, :], 1.0, 0.0).astype(BF)
 
     first = (b * 64 + me) * LEAF_DEV - HALO
 
@@ -240,14 +243,12 @@
             LEAF_DEV, 4, 16, NRHS
         )
 
-    tall_row = lax.broadcasted_iota(jnp.int32, (256, 256), 0).astype(F32)
 
     def slots(i, h):
         region = xr.at[i, pl.ds(2 * h, 2), pl.ds(0, 7)]
         pltpu.make_async_copy(region, region, xr_sem.at[i, h]).wait()
-        hot = jnp.where(tall_row == vrow[i:i + 1, :], 1.0, 0.0).astype(BF)
         blocks = jnp.concatenate([xr[i, 2 * h + q].reshape(256, NRHS) for q in range(2)], axis=1)
-        sums = dot(hot, blocks)
+        sums = dot(hots[i], blocks)
         return [sums[:, q * NRHS:(q + 1) * NRHS] for q in range(2)]
 
     def z_copy(i, h, sign):
@@ -369,6 +370,7 @@
             pltpu.VMEM((8, 8, 4, 32, NRHS), BF),
             pltpu.VMEM((8, 4, 8, 32, NRHS), BF),
             pltpu.VMEM((16, 256), F32),
+            pltpu.VMEM((8, 256, 256), BF),
             pltpu.VMEM((7, 2, 2, 256, NRHS), BF),
             pltpu.VMEM((7, 2, 2, 256, NRHS), BF),
             pltpu.VMEM((RANK, NRHS), BF),

time: 37.2 us -> 37.2 us (level)
  no operation moved by 1% of the time
where the time goes in v6:
time: 37.2 us; the launch traced here: 37.1 us
  Pallas kernels  36.4 us (98%)
  local copies, waits for them, and re-layouts  0.71 us (2%)
    pallas_call x1, Pallas kernels, per_device(): pl.pallas_call(kernel, name='adjoint', out_shape=pltpu.VMEM((LEAF_DEV, LE...  36.4 us

profile of v6, /device:TPU:1, one launch (start us, length us, event | category | flops | bytes accessed | tf_op | source)
XLA Modules:
  0.0 37.1 jit_solution(3581451540651796323)
XLA Ops:
  0.0 36.4 %adjoint.1 = bf16[16,64,128]{2,1,0:T(8,128)(2,1)S(1)} custom-call(s32[3,16]{1,0:T(4,128)} %bitcast.6, s32[3,16]{1,0:T(4,128)} %bitcast.7, s32[16,12]{1,0:T(8,128)} %ns_hbm.1, s32[1,2]{1,0:T(1,128)} %us_hbm.1, bf16[16,64,128]{2,1,0:T(8,128)(2,1)} %bitcast.5, bf16[16,64,768]{2,1,0:T(8,128)(2,1)} %near_block.1, bf16[16,64,128]{2,1,0:T(8,128)(2,1)} %bases.1, ...), custom_call_target="tpu_custom_call" | custom-call | tf_op jit(solution)/shard_map/adjoint/pallas_call | solution.py:347
  36.4 0.7 %copy.12 = bf16[1024,128]{1,0:T(8,128)(2,1)} copy(bf16[1024,128]{1,0:T(8,128)(2,1)S(1)} %bitcast.4) | data formatting | bytes 524288
